TPU v7x, 512 devices: a whole 4x4x16 slice. The times are simulated.
512 devices in a mesh: seq: 128 (over z, x, core), head: 4 (over y).
Axes of the slice: x: 4, y: 4, z: 16, core: 2. Of those that a mesh axis runs over, the one named last changes fastest.
Arguments:
- queries: bfloat16 [32768, 512], P('seq', 'head'), may hold values from -16 to 16
- keys: bfloat16 [32768, 512], P('seq', 'head'), may hold values from -16 to 16
- values: bfloat16 [32768, 512], P('seq', 'head'), may hold values from -16 to 16
- out_weight: bfloat16 [512, 512], replicated, may hold values from -0.5 to 0.5
Outputs:
- mixed: bfloat16 [32768, 512], P(('seq', 'head'))
All inputs are finite; a program needn't handle non-finite values.
Results may differ from a plain program's by a relative error of at most 0.00185.
The roundings to bfloat16 on the way count: a program that leaves them out, or rounds other values in their place, can miss the bound.
Values may be sent and summed in bfloat16 or wider, within the bound.
A program may use at most 128 MiB of HBM per device.

v0:
```python
import math
import jax
import jax.numpy as jnp
from jax import lax
from jax.sharding import PartitionSpec as P

HD = 64
LEAF = 128


def extended_2(cells, sides, width):
    for axis, dim in sides:
        count = lax.axis_size(axis)
        ends = count - 1
        head = lax.slice_in_dim(cells, 0, width, axis=dim)
        tail = lax.slice_in_dim(cells, cells.shape[dim] - width, cells.shape[dim], axis=dim)
        cells = jnp.concatenate(
            [
                lax.ppermute(tail, axis, [(i, (i + 1) % count) for i in range(ends)]),
                cells,
                lax.ppermute(head, axis, [((i + 1) % count, i) for i in range(ends)]),
            ],
            axis=dim,
        )
    return cells


def as_sent(x):

    def short(part):
        return part.astype(jnp.bfloat16) if part.dtype == jnp.float32 else part

    return jax.tree.map(short, x)


def average_pairs(stacked):
    widened = stacked.astype(jnp.float32).reshape(2, stacked.shape[1] // 2, 2, stacked.shape[2])
    return (0.5 * (widened[:, :, 0] + widened[:, :, 1])).astype(jnp.bfloat16)


def near_set(leaf, extended, seq_index, blocks_dev, seq_size):
    positions = jnp.arange(LEAF, dtype=jnp.int32)
    upper_half = positions >= LEAF // 2
    global_leaf = seq_index * blocks_dev + leaf
    all_blocks = seq_size * blocks_dev
    key_parts = [lax.dynamic_slice_in_dim(extended[0], leaf * LEAF, 3 * LEAF, 1)]
    neighbour = global_leaf - 1 + jnp.arange(3 * LEAF, dtype=jnp.int32) // LEAF
    valid_parts = [(neighbour >= 0) & (neighbour < all_blocks)]
    local_block = leaf >> 1
    global_block = global_leaf >> 1
    parity = global_leaf >> 0 & 1
    level_blocks = all_blocks >> 1
    key_parts.append(lax.dynamic_slice_in_dim(extended[1], local_block * LEAF, LEAF, 1))
    key_parts.append(lax.dynamic_slice_in_dim(extended[1], (local_block + 2) * LEAF, LEAF, 1))
    valid_parts.append((global_block >= 1) & jnp.logical_not(upper_half & (parity == 0)))
    valid_parts.append(
        (global_block + 1 < level_blocks)
        & jnp.logical_not(jnp.logical_not(upper_half) & (parity == 1))
    )
    return (jnp.concatenate(key_parts, axis=1), jnp.concatenate(valid_parts, axis=0))


def shards(queries, keys, values, out_weight):
    tok_count = queries.shape[0]
    width = queries.shape[1]
    seq_size = lax.axis_size("seq")
    seq_index = lax.axis_index("seq")
    blocks_dev = tok_count // LEAF
    near_count = blocks_dev.bit_length() - 1
    far_count = max(0, seq_size.bit_length() - 2)
    scale = 1.0 / math.sqrt(HD)
    positions = jnp.arange(LEAF, dtype=jnp.int32)
    upper_half = positions >= LEAF // 2
    local = [jnp.stack([keys, values], axis=0)]
    local.append(average_pairs(local[-1]))
    extended = [extended_2(stacked, (("seq", 1),), LEAF) for stacked in local]
    own_block = local[near_count]
    far_pairs = []
    far_valid = []
    everything = lax.all_gather(own_block, "seq", axis=1, tiled=True)
    for level_far in range(1, far_count + 1):
        everything = average_pairs(everything)
        group = seq_index >> level_far
        padded = jnp.pad(everything, ((0, 0), (LEAF, LEAF), (0, 0)))
        lower = lax.dynamic_slice_in_dim(padded, group * LEAF, LEAF, 1)
        upper = lax.dynamic_slice_in_dim(padded, (group + 2) * LEAF, LEAF, 1)
        far_pairs.append(jnp.concatenate([lower, upper], axis=1))
    for level_far in range(1, far_count + 1):
        group = seq_index >> level_far
        parity = seq_index >> level_far - 1 & 1
        far_valid.append((group >= 1) & jnp.logical_not(upper_half & (parity == 0)))
        far_valid.append(
            (group + 1 < seq_size >> level_far)
            & jnp.logical_not(jnp.logical_not(upper_half) & (parity == 1))
        )
    far_keys = jnp.concatenate(far_pairs, axis=1)
    far_mask = jnp.concatenate(far_valid, axis=0)
    leaves_step = min(blocks_dev, max(1, 512 // LEAF))
    step_count = blocks_dev // leaves_step

    def attend(step):
        leaves = step * leaves_step + jnp.arange(leaves_step, dtype=jnp.int32)
        near_keys, near_mask = jax.vmap(
            lambda leaf: near_set(leaf, extended, seq_index, blocks_dev, seq_size)
        )(leaves)
        query_block = queries.reshape(leaves_step, LEAF, width)
        head_outputs = []
        for head_number in range(width // HD):
            low_col = head_number * HD
            high_col = low_col + HD
            near_scores = (
                jnp.einsum(
                    "nhs,nos->nho",
                    query_block[:, :, low_col:high_col],
                    near_keys[:, 0, :, low_col:high_col],
                    preferred_element_type=jnp.float32,
                )
                * scale
            )
            near_scores = jnp.where(near_mask[:, None, :], near_scores, -jnp.inf)
            peak = jnp.max(near_scores, axis=-1, keepdims=True)
            far_scores = (
                jnp.einsum(
                    "qs,os->qo",
                    queries[:, low_col:high_col],
                    far_keys[0, :, low_col:high_col],
                    preferred_element_type=jnp.float32,
                )
                * scale
            )
            far_scores = far_scores.reshape(leaves_step, LEAF, far_scores.shape[-1])
            far_scores = jnp.where(far_mask[None, None, :], far_scores, -jnp.inf)
            peak = jnp.maximum(peak, jnp.max(far_scores, axis=-1, keepdims=True))
            near_weights = jnp.exp(near_scores - peak)
            total = jnp.sum(near_weights, axis=-1)
            numer = jnp.einsum(
                "fkm,fmp->fkp",
                near_weights.astype(jnp.bfloat16),
                near_keys[:, 1, :, low_col:high_col],
                preferred_element_type=jnp.float32,
            )
            far_weights = jnp.exp(far_scores - peak)
            total = total + jnp.sum(far_weights, axis=-1)
            far_rounded = far_weights.astype(jnp.bfloat16).reshape(
                leaves_step * LEAF, far_weights.shape[-1]
            )
            far_numer = jnp.dot(
                far_rounded, far_keys[1, :, low_col:high_col], preferred_element_type=jnp.float32
            )
            numer = numer + far_numer.reshape(leaves_step, LEAF, HD)
            head_outputs.append((numer / total[..., None]).astype(jnp.bfloat16))
        return jnp.concatenate(head_outputs, axis=-1).reshape(leaves_step * LEAF, width)

    attended = lax.map(attend, jnp.arange(step_count, dtype=jnp.int32)).reshape(tok_count, width)
    gathered_rows = lax.all_to_all(
        as_sent(attended), "head", split_axis=0, concat_axis=1, tiled=True
    ).astype(attended.dtype)
    return jnp.dot(gathered_rows, out_weight, preferred_element_type=jnp.float32).astype(
        jnp.bfloat16
    )


def solution(mesh):
    in_specs = (P("seq", "head"), P("seq", "head"), P("seq", "head"), P())
    out_specs = P(("seq", "head"), None)
    return jax.shard_map(shards, mesh=mesh, in_specs=in_specs, out_specs=out_specs, check_vma=False)
```

profile of v0, /device:TPU:32, one launch (start us, length us, event | category | flops | bytes accessed | tf_op | source)
XLA Modules:
  0.0 354.0 jit_solution(11749175016474953703)
XLA Ops:
  11.6 5.8 %collective-permute-start.3 = (bf16[2,128,128]{2,0,1:T(2,128)(2,1)S(1)}, bf16[2,128,128]{2,0,1:T(2,128)(2,1)S(1)}, u32[]{:S(2)}, u32[]{:S(2)}) collective-permute-start(bf16[2,128,128]{2,0,1:T(2,128)(2,1)S(1)} %fusion.76), channel_id=1, source_target_pairs={{4,0},{8,4},{12,8},{16,12},{20,16},{24,20},{28,24},{32,28},{36,32}... | collective-permute-start | bytes 196616 | tf_op jit(solution)/shard_map/ppermute | solution.py:21
  21.4 5.8 %collective-permute-start.1 = (bf16[2,128,128]{2,0,1:T(2,128)(2,1)S(1)}, bf16[2,128,128]{2,0,1:T(2,128)(2,1)S(1)}, u32[]{:S(2)}, u32[]{:S(2)}) collective-permute-start(bf16[2,128,128]{2,0,1:T(2,128)(2,1)S(1)} %get-tuple-element.46), channel_id=1, source_target_pairs={{4,0},{8,4},{12,8},{16,12},{20,16},{24,20},{28,24},{32,28},{36,32}... | collective-permute-start | bytes 196616 | tf_op jit(solution)/shard_map/ppermute | solution.py:21
  37.7 124.1 %all-gather.3.cloned.1.call-done = bf16[2,16384,1,128]{3,0,2,1:T(2,128)(2,1)} async-done(((bf16[2,128,1,128]{3,0,2,1:T(2,128)(2,1)}), bf16[2,16384,1,128]{3,0,2,1:T(2,128)(2,1)}) %all-gather.3.cloned.1.call-update) | async-done | bytes 8388624 | tf_op jit(solution)/shard_map/all_gather | solution.py:80
  161.8 5.1 %copy.50 = bf16[2,16384,1,128]{3,1,0,2:T(8,128)(2,1)S(1)} copy(bf16[2,16384,1,128]{3,0,2,1:T(2,128)(2,1)} %all-gather.3.cloned.1.call-done) | data formatting | bytes 16777216 | tf_op jit(solution)/shard_map/all_gather | solution.py:80
  166.8 13.0 %fusion.63 = (f32[2,8192,1,128]{3,2,1,0:T(1,128)}, f32[2,8192,1,128]{3,2,1,0:T(1,128)}) fusion(bf16[2,8192,2,128]{3,2,1,0:T(2,128)(2,1)S(1)} %bitcast.97), kind=kLoop, calls=%fused_computation.146 | loop fusion | bytes 33554432 | tf_op jit(solution)/shard_map/slice | solution.py:38
  179.8 18.0 %copy.76 = f32[2,8192,1,128]{1,3,0,2:T(8,128)} copy(f32[2,8192,1,128]{3,2,1,0:T(1,128)} %get-tuple-element.22) | data formatting | bytes 16777216
  197.8 18.0 %copy.77 = f32[2,8192,1,128]{1,3,0,2:T(8,128)} copy(f32[2,8192,1,128]{3,2,1,0:T(1,128)} %get-tuple-element.21) | data formatting | bytes 16777216
  215.8 9.4 %multiply_convert_fusion = bf16[2,8192,1,128]{1,3,0,2:T(8,128)(2,1)} fusion(f32[2,8192,1,128]{1,3,0,2:T(8,128)} %copy.76, f32[2,8192,1,128]{1,3,0,2:T(8,128)} %copy.77), kind=kLoop, calls=%fused_computation.3 | loop fusion | flops 6291456 | bytes 20971520 | tf_op jit(solution)/shard_map/convert_element_type | solution.py:38
  225.2 7.0 %copy.53 = f32[2,8192,1,128]{3,1,0,2:T(8,128)} copy(bf16[2,8192,1,128]{1,3,0,2:T(8,128)(2,1)} %multiply_convert_fusion) | data formatting | bytes 12582912 | tf_op jit(solution)/shard_map/convert_element_type | solution.py:37
  232.3 11.5 %fusion.62 = (f32[2,4096,1,128]{3,2,1,0:T(1,128)}, f32[2,4096,1,128]{3,2,1,0:T(1,128)}) fusion(f32[2,4096,2,128]{3,2,1,0:T(2,128)} %bitcast.102), kind=kLoop, calls=%fused_computation.145 | loop fusion | bytes 16777216 | tf_op jit(solution)/shard_map/slice | solution.py:38
  243.8 10.2 %copy.78 = f32[2,4096,1,128]{1,3,0,2:T(8,128)} copy(f32[2,4096,1,128]{3,2,1,0:T(1,128)} %get-tuple-element.20) | data formatting | bytes 8388608
  254.0 10.2 %copy.79 = f32[2,4096,1,128]{1,3,0,2:T(8,128)} copy(f32[2,4096,1,128]{3,2,1,0:T(1,128)} %get-tuple-element.19) | data formatting | bytes 8388608
  264.1 4.3 %multiply_convert_fusion.1 = bf16[2,4096,1,128]{1,3,0,2:T(8,128)(2,1)S(1)} fusion(f32[2,4096,1,128]{1,3,0,2:T(8,128)} %copy.78, f32[2,4096,1,128]{1,3,0,2:T(8,128)} %copy.79), kind=kLoop, calls=%fused_computation.4 | loop fusion | flops 3145728 | bytes 10485760 | tf_op jit(solution)/shard_map/convert_element_type | solution.py:38
  268.5 2.9 copy.56
  271.4 7.9 %fusion.64 = (f32[2,2048,1,128]{3,2,1,0:T(1,128)}, f32[2,2048,1,128]{3,2,1,0:T(1,128)}) fusion(f32[2,2048,2,128]{3,2,1,0:T(2,128)} %bitcast.105), kind=kLoop, calls=%fused_computation.147 | loop fusion | bytes 8388608 | tf_op jit(solution)/shard_map/slice | solution.py:38
  279.3 6.1 %copy.80 = f32[2,2048,1,128]{1,3,0,2:T(8,128)} copy(f32[2,2048,1,128]{3,2,1,0:T(1,128)} %get-tuple-element.32) | data formatting | bytes 4194304
  285.4 6.1 %copy.81 = f32[2,2048,1,128]{1,3,0,2:T(8,128)} copy(f32[2,2048,1,128]{3,2,1,0:T(1,128)} %get-tuple-element.23) | data formatting | bytes 4194304
  291.5 3.6 %multiply_convert_fusion.2 = bf16[2,2048,1,128]{1,3,0,2:T(8,128)(2,1)} fusion(f32[2,2048,1,128]{1,3,0,2:T(8,128)} %copy.80, f32[2,2048,1,128]{1,3,0,2:T(8,128)} %copy.81), kind=kLoop, calls=%fused_computation.11 | loop fusion | flops 1572864 | bytes 5242880 | tf_op jit(solution)/shard_map/convert_element_type | solution.py:38
  295.1 2.6 copy.59
  297.7 5.4 %fusion.65 = (f32[2,1024,1,128]{3,2,1,0:T(1,128)}, f32[2,1024,1,128]{3,2,1,0:T(1,128)}) fusion(f32[2,1024,2,128]{3,2,1,0:T(2,128)} %bitcast.108), kind=kLoop, calls=%fused_computation.148 | loop fusion | bytes 4194304 | tf_op jit(solution)/shard_map/slice | solution.py:38
  303.1 3.6 %copy.82 = f32[2,1024,1,128]{1,3,0,2:T(8,128)} copy(f32[2,1024,1,128]{3,2,1,0:T(1,128)} %get-tuple-element.36) | data formatting | bytes 2097152
  306.7 3.6 %copy.83 = f32[2,1024,1,128]{1,3,0,2:T(8,128)} copy(f32[2,1024,1,128]{3,2,1,0:T(1,128)} %get-tuple-element.34) | data formatting | bytes 2097152
  313.3 3.5 fusion.66
  336.6 9.7 %all_to_all.19 = bf16[4,64,128]{2,1,0:T(8,128)(2,1)S(1)} all-to-all(bf16[4,64,128]{2,1,0:T(8,128)(2,1)S(1)} %bitcast.121), channel_id=1, replica_groups=mesh['seq'=128,'head'=4] {'head'}, dimensions={0} | all-to-all | bytes 131072 | tf_op jit(solution)/shard_map/all_to_all | solution.py:155
  (125 shorter events, 42.7 us)
Async XLA Ops:
  6.5 339.8 %copy-start = (bf16[512,512]{1,0:T(8,128)(2,1)S(1)}, bf16[512,512]{1,0:T(8,128)(2,1)}, u32[]{:S(2)}) copy-start(bf16[512,512]{1,0:T(8,128)(2,1)} %param.7) | copy-start | bytes 1572868
  6.5 155.2 %all-gather.3.cloned.1.call-start = ((), (), s32[]{:S(2)}) async-start(), calls=%async_computation.1 | async-start | bytes 8454144 | tf_op jit(solution)/shard_map/all_gather | solution.py:80
  9.6 21.1 %collective-permute-start.2 = (bf16[2,128,128]{2,0,1:T(2,128)(2,1)S(1)}, bf16[2,128,128]{2,0,1:T(2,128)(2,1)S(1)}, u32[]{:S(2)}, u32[]{:S(2)}) collective-permute-start(bf16[2,128,128]{2,0,1:T(2,128)(2,1)S(1)} %fusion.76), channel_id=1, source_target_pairs={{0,4},{4,8},{8,12},{12,16},{16,20},{20,24},{24,28},{28,32},{32,36}... | collective-permute-start | bytes 196616 | tf_op jit(solution)/shard_map/ppermute | solution.py:19
  11.6 19.1 %collective-permute-start.3 = (bf16[2,128,128]{2,0,1:T(2,128)(2,1)S(1)}, bf16[2,128,128]{2,0,1:T(2,128)(2,1)S(1)}, u32[]{:S(2)}, u32[]{:S(2)}) collective-permute-start(bf16[2,128,128]{2,0,1:T(2,128)(2,1)S(1)} %fusion.76), channel_id=1, source_target_pairs={{4,0},{8,4},{12,8},{16,12},{20,16},{24,20},{28,24},{32,28},{36,32}... | collective-permute-start | bytes 196616 | tf_op jit(solution)/shard_map/ppermute | solution.py:21
  19.5 13.4 %collective-permute-start = (bf16[2,128,128]{2,0,1:T(2,128)(2,1)S(1)}, bf16[2,128,128]{2,0,1:T(2,128)(2,1)S(1)}, u32[]{:S(2)}, u32[]{:S(2)}) collective-permute-start(bf16[2,128,128]{2,0,1:T(2,128)(2,1)S(1)} %get-tuple-element.45), channel_id=1, source_target_pairs={{0,4},{4,8},{8,12},{12,16},{16,20},{20,24},{24,28},{28,32},{32,36}... | collective-permute-start | bytes 196616 | tf_op jit(solution)/shard_map/ppermute | solution.py:19
  21.4 11.5 %collective-permute-start.1 = (bf16[2,128,128]{2,0,1:T(2,128)(2,1)S(1)}, bf16[2,128,128]{2,0,1:T(2,128)(2,1)S(1)}, u32[]{:S(2)}, u32[]{:S(2)}) collective-permute-start(bf16[2,128,128]{2,0,1:T(2,128)(2,1)S(1)} %get-tuple-element.46), channel_id=1, source_target_pairs={{4,0},{8,4},{12,8},{16,12},{20,16},{24,20},{28,24},{32,28},{36,32}... | collective-permute-start | bytes 196616 | tf_op jit(solution)/shard_map/ppermute | solution.py:21
  32.0 3.3 copy-start.9
  35.2 1.2 copy-start.5
  328.9 2.2 copy-start.1
  331.2 1.2 copy-start.2
  331.3 1.4 copy-start.7
  331.3 1.4 copy-start.8
  332.5 1.1 copy-start.4
  332.6 1.2 copy-start.6
  333.3 1.3 copy-start.3
Sparse Core Ops, SparseCore 0:
  10.5 151.2 all-gather.2
where the time goes:
time: 357 us; the launch traced here: 354 us
  local copies, waits for them, and re-layouts  161 us (45%)
  waiting for transfers between devices  124 us (35%)
  other arithmetic  24 us (7%)
  starting transfers between devices  15.3 us (4%)
  between operations  14 us (4%)
  blocking collectives  9.71 us (3%)
  matrix products  5.36 us (2%)
    all_gather x1, waiting for transfers between devices, shards(): everything = lax.all_gather(own_block, 'seq', axis=1, tiled=True)  124 us
    unnamed x54, local copies, waits for them, and re-layouts  90 us
    slice x6, local copies, waits for them, and re-layouts, average_pairs(): return (0.5 * (widened[:, :, 0] + widened[:, :, 1])).astype(jnp.bfloat16)  43.9 us
    convert_element_type x8, other arithmetic, average_pairs(): return (0.5 * (widened[:, :, 0] + widened[:, :, 1])).astype(jnp.bfloat16)  21.3 us
    convert_element_type x5, local copies, waits for them, and re-layouts, average_pairs(): stacked.astype(jnp.float32)  14.7 us
    ppermute x2, starting transfers between devices, extended_2(): lax.ppermute(head, axis, [((i + 1) % count, i) for i in range(ends)])  11.5 us
    all_to_all x1, blocking collectives, shards(): lax.all_to_all(as_sent(attended), 'head', split_axis=0, concat_axis=1, ti...  9.71 us
  transfers between devices with their start and end apart: 5, of which 1 were waited for; matrix products, arithmetic and copies ran while one was open for 4% of the time, Pallas kernels for 0%

commit v1 on v0

--- a/solution.py
+++ b/solution.py
@@ -1,3 +1,4 @@
+import functools
 import math
 import jax
 import jax.numpy as jnp
@@ -6,6 +7,17 @@
 
 HD = 64
 LEAF = 128
+
+
+def ticks_choose(vector, axis_name, dim_i, which_dim):
+    low = lax.psum(1, axis_name)
+    aux = jnp.split(vector, low, dim_i)
+    reply = jnp.stack(aux, 0)
+    local_part = lax.all_to_all(reply, axis_name, 0, 0)
+    return jnp.concatenate(local_part, which_dim)
+
+
+_close_frame = functools.partial(ticks_choose, axis_name="head", dim_i=0, which_dim=1)
 
 
 def extended_2(cells, sides, width):
@@ -152,9 +164,7 @@
         return jnp.concatenate(head_outputs, axis=-1).reshape(leaves_step * LEAF, width)
 
     attended = lax.map(attend, jnp.arange(step_count, dtype=jnp.int32)).reshape(tok_count, width)
-    gathered_rows = lax.all_to_all(
-        as_sent(attended), "head", split_axis=0, concat_axis=1, tiled=True
-    ).astype(attended.dtype)
+    gathered_rows = _close_frame(as_sent(attended)).astype(attended.dtype)
     return jnp.dot(gathered_rows, out_weight, preferred_element_type=jnp.float32).astype(
         jnp.bfloat16
     )

time: 357 us -> 357 us (level)
  no operation moved by 1% of the time
where the time goes in v1:
time: 357 us; the launch traced here: 354 us
  local copies, waits for them, and re-layouts  162 us (45%)
  waiting for transfers between devices  124 us (35%)
  other arithmetic  24.1 us (7%)
  starting transfers between devices  15.3 us (4%)
  between operations  14 us (4%)
  blocking collectives  9.72 us (3%)
  matrix products  5.34 us (1%)
    all_gather x1, waiting for transfers between devices, shards(): everything = lax.all_gather(own_block, 'seq', axis=1, tiled=True)  124 us
    unnamed x54, local copies, waits for them, and re-layouts  90.1 us
    slice x6, local copies, waits for them, and re-layouts, average_pairs(): return (0.5 * (widened[:, :, 0] + widened[:, :, 1])).astype(jnp.bfloat16)  43.9 us
    convert_element_type x8, other arithmetic, average_pairs(): return (0.5 * (widened[:, :, 0] + widened[:, :, 1])).astype(jnp.bfloat16)  21.3 us
    convert_element_type x5, local copies, waits for them, and re-layouts, average_pairs(): stacked.astype(jnp.float32)  14.7 us
    ppermute x2, starting transfers between devices, extended_2(): lax.ppermute(head, axis, [((i + 1) % count, i) for i in range(ends)])  11.5 us
    all_to_all x1, blocking collectives, ticks_choose(): local_part = lax.all_to_all(reply, axis_name, 0, 0)  9.72 us
  transfers between devices with their start and end apart: 5, of which 1 were waited for; matrix products, arithmetic and copies ran while one was open for 4% of the time, Pallas kernels for 0%

profile of v1, /device:TPU:32, one launch (start us, length us, event | category | flops | bytes accessed | tf_op | source)
XLA Modules:
  0.0 354.2 jit_solution(13869838341721586421)
XLA Ops:
  11.6 5.8 %collective-permute-start.3 = (bf16[2,128,128]{2,0,1:T(2,128)(2,1)S(1)}, bf16[2,128,128]{2,0,1:T(2,128)(2,1)S(1)}, u32[]{:S(2)}, u32[]{:S(2)}) collective-permute-start(bf16[2,128,128]{2,0,1:T(2,128)(2,1)S(1)} %fusion.76), channel_id=1, source_target_pairs={{4,0},{8,4},{12,8},{16,12},{20,16},{24,20},{28,24},{32,28},{36,32}... | collective-permute-start | bytes 196616 | tf_op jit(solution)/shard_map/ppermute | solution.py:33
  21.4 5.8 %collective-permute-start.1 = (bf16[2,128,128]{2,0,1:T(2,128)(2,1)S(1)}, bf16[2,128,128]{2,0,1:T(2,128)(2,1)S(1)}, u32[]{:S(2)}, u32[]{:S(2)}) collective-permute-start(bf16[2,128,128]{2,0,1:T(2,128)(2,1)S(1)} %get-tuple-element.46), channel_id=1, source_target_pairs={{4,0},{8,4},{12,8},{16,12},{20,16},{24,20},{28,24},{32,28},{36,32}... | collective-permute-start | bytes 196616 | tf_op jit(solution)/shard_map/ppermute | solution.py:33
  37.7 124.1 %all-gather.3.cloned.1.call-done = bf16[2,16384,1,128]{3,0,2,1:T(2,128)(2,1)} async-done(((bf16[2,128,1,128]{3,0,2,1:T(2,128)(2,1)}), bf16[2,16384,1,128]{3,0,2,1:T(2,128)(2,1)}) %all-gather.3.cloned.1.call-update) | async-done | bytes 8388624 | tf_op jit(solution)/shard_map/all_gather | solution.py:92
  161.8 5.1 %copy.50 = bf16[2,16384,1,128]{3,1,0,2:T(8,128)(2,1)S(1)} copy(bf16[2,16384,1,128]{3,0,2,1:T(2,128)(2,1)} %all-gather.3.cloned.1.call-done) | data formatting | bytes 16777216 | tf_op jit(solution)/shard_map/all_gather | solution.py:92
  166.8 13.0 %fusion.63 = (f32[2,8192,1,128]{3,2,1,0:T(1,128)}, f32[2,8192,1,128]{3,2,1,0:T(1,128)}) fusion(bf16[2,8192,2,128]{3,2,1,0:T(2,128)(2,1)S(1)} %bitcast.105), kind=kLoop, calls=%fused_computation.151 | loop fusion | bytes 33554432 | tf_op jit(solution)/shard_map/slice | solution.py:50
  179.8 18.0 %copy.76 = f32[2,8192,1,128]{1,3,0,2:T(8,128)} copy(f32[2,8192,1,128]{3,2,1,0:T(1,128)} %get-tuple-element.22) | data formatting | bytes 16777216
  197.9 18.1 %copy.77 = f32[2,8192,1,128]{1,3,0,2:T(8,128)} copy(f32[2,8192,1,128]{3,2,1,0:T(1,128)} %get-tuple-element.21) | data formatting | bytes 16777216
  215.9 9.4 %multiply_convert_fusion = bf16[2,8192,1,128]{1,3,0,2:T(8,128)(2,1)} fusion(f32[2,8192,1,128]{1,3,0,2:T(8,128)} %copy.76, f32[2,8192,1,128]{1,3,0,2:T(8,128)} %copy.77), kind=kLoop, calls=%fused_computation.3 | loop fusion | flops 6291456 | bytes 20971520 | tf_op jit(solution)/shard_map/convert_element_type | solution.py:50
  225.3 7.0 %copy.53 = f32[2,8192,1,128]{3,1,0,2:T(8,128)} copy(bf16[2,8192,1,128]{1,3,0,2:T(8,128)(2,1)} %multiply_convert_fusion) | data formatting | bytes 12582912 | tf_op jit(solution)/shard_map/convert_element_type | solution.py:49
  232.4 11.5 %fusion.62 = (f32[2,4096,1,128]{3,2,1,0:T(1,128)}, f32[2,4096,1,128]{3,2,1,0:T(1,128)}) fusion(f32[2,4096,2,128]{3,2,1,0:T(2,128)} %bitcast.110), kind=kLoop, calls=%fused_computation.150 | loop fusion | bytes 16777216 | tf_op jit(solution)/shard_map/slice | solution.py:50
  243.9 10.2 %copy.78 = f32[2,4096,1,128]{1,3,0,2:T(8,128)} copy(f32[2,4096,1,128]{3,2,1,0:T(1,128)} %get-tuple-element.20) | data formatting | bytes 8388608
  254.1 10.1 %copy.79 = f32[2,4096,1,128]{1,3,0,2:T(8,128)} copy(f32[2,4096,1,128]{3,2,1,0:T(1,128)} %get-tuple-element.19) | data formatting | bytes 8388608
  264.2 4.3 %multiply_convert_fusion.1 = bf16[2,4096,1,128]{1,3,0,2:T(8,128)(2,1)S(1)} fusion(f32[2,4096,1,128]{1,3,0,2:T(8,128)} %copy.78, f32[2,4096,1,128]{1,3,0,2:T(8,128)} %copy.79), kind=kLoop, calls=%fused_computation.4 | loop fusion | flops 3145728 | bytes 10485760 | tf_op jit(solution)/shard_map/convert_element_type | solution.py:50
  268.6 2.9 copy.56
  271.5 8.0 %fusion.64 = (f32[2,2048,1,128]{3,2,1,0:T(1,128)}, f32[2,2048,1,128]{3,2,1,0:T(1,128)}) fusion(f32[2,2048,2,128]{3,2,1,0:T(2,128)} %bitcast.113), kind=kLoop, calls=%fused_computation.152 | loop fusion | bytes 8388608 | tf_op jit(solution)/shard_map/slice | solution.py:50
  279.5 6.1 %copy.80 = f32[2,2048,1,128]{1,3,0,2:T(8,128)} copy(f32[2,2048,1,128]{3,2,1,0:T(1,128)} %get-tuple-element.32) | data formatting | bytes 4194304
  285.6 6.0 %copy.81 = f32[2,2048,1,128]{1,3,0,2:T(8,128)} copy(f32[2,2048,1,128]{3,2,1,0:T(1,128)} %get-tuple-element.23) | data formatting | bytes 4194304
  291.6 3.6 %multiply_convert_fusion.2 = bf16[2,2048,1,128]{1,3,0,2:T(8,128)(2,1)} fusion(f32[2,2048,1,128]{1,3,0,2:T(8,128)} %copy.80, f32[2,2048,1,128]{1,3,0,2:T(8,128)} %copy.81), kind=kLoop, calls=%fused_computation.11 | loop fusion | flops 1572864 | bytes 5242880 | tf_op jit(solution)/shard_map/convert_element_type | solution.py:50
  295.3 2.6 copy.59
  297.8 5.4 %fusion.65 = (f32[2,1024,1,128]{3,2,1,0:T(1,128)}, f32[2,1024,1,128]{3,2,1,0:T(1,128)}) fusion(f32[2,1024,2,128]{3,2,1,0:T(2,128)} %bitcast.116), kind=kLoop, calls=%fused_computation.153 | loop fusion | bytes 4194304 | tf_op jit(solution)/shard_map/slice | solution.py:50
  303.3 3.6 %copy.82 = f32[2,1024,1,128]{1,3,0,2:T(8,128)} copy(f32[2,1024,1,128]{3,2,1,0:T(1,128)} %get-tuple-element.36) | data formatting | bytes 2097152
  306.9 3.6 %copy.83 = f32[2,1024,1,128]{1,3,0,2:T(8,128)} copy(f32[2,1024,1,128]{3,2,1,0:T(1,128)} %get-tuple-element.34) | data formatting | bytes 2097152
  313.5 3.5 fusion.66
  336.8 9.7 %all_to_all.5 = bf16[4,64,128]{2,1,0:T(8,128)(2,1)S(1)} all-to-all(bf16[4,64,128]{2,1,0:T(8,128)(2,1)S(1)} %pad_maximum_fusion.5), channel_id=1, replica_groups=mesh['seq'=128,'head'=4] {'head'}, dimensions={0} | all-to-all | bytes 131072 | tf_op jit(solution)/shard_map/all_to_all | solution.py:16
  (127 shorter events, 42.7 us)
Async XLA Ops:
  6.5 340.0 %copy-start = (bf16[512,512]{1,0:T(8,128)(2,1)S(1)}, bf16[512,512]{1,0:T(8,128)(2,1)}, u32[]{:S(2)}) copy-start(bf16[512,512]{1,0:T(8,128)(2,1)} %param.7) | copy-start | bytes 1572868
  6.5 155.2 %all-gather.3.cloned.1.call-start = ((), (), s32[]{:S(2)}) async-start(), calls=%async_computation.1 | async-start | bytes 8454144 | tf_op jit(solution)/shard_map/all_gather | solution.py:92
  9.6 21.1 %collective-permute-start.2 = (bf16[2,128,128]{2,0,1:T(2,128)(2,1)S(1)}, bf16[2,128,128]{2,0,1:T(2,128)(2,1)S(1)}, u32[]{:S(2)}, u32[]{:S(2)}) collective-permute-start(bf16[2,128,128]{2,0,1:T(2,128)(2,1)S(1)} %fusion.76), channel_id=1, source_target_pairs={{0,4},{4,8},{8,12},{12,16},{16,20},{20,24},{24,28},{28,32},{32,36}... | collective-permute-start | bytes 196616 | tf_op jit(solution)/shard_map/ppermute | solution.py:31
  11.6 19.1 %collective-permute-start.3 = (bf16[2,128,128]{2,0,1:T(2,128)(2,1)S(1)}, bf16[2,128,128]{2,0,1:T(2,128)(2,1)S(1)}, u32[]{:S(2)}, u32[]{:S(2)}) collective-permute-start(bf16[2,128,128]{2,0,1:T(2,128)(2,1)S(1)} %fusion.76), channel_id=1, source_target_pairs={{4,0},{8,4},{12,8},{16,12},{20,16},{24,20},{28,24},{32,28},{36,32}... | collective-permute-start | bytes 196616 | tf_op jit(solution)/shard_map/ppermute | solution.py:33
  19.5 13.4 %collective-permute-start = (bf16[2,128,128]{2,0,1:T(2,128)(2,1)S(1)}, bf16[2,128,128]{2,0,1:T(2,128)(2,1)S(1)}, u32[]{:S(2)}, u32[]{:S(2)}) collective-permute-start(bf16[2,128,128]{2,0,1:T(2,128)(2,1)S(1)} %get-tuple-element.45), channel_id=1, source_target_pairs={{0,4},{4,8},{8,12},{12,16},{16,20},{20,24},{24,28},{28,32},{32,36}... | collective-permute-start | bytes 196616 | tf_op jit(solution)/shard_map/ppermute | solution.py:31
  21.4 11.5 %collective-permute-start.1 = (bf16[2,128,128]{2,0,1:T(2,128)(2,1)S(1)}, bf16[2,128,128]{2,0,1:T(2,128)(2,1)S(1)}, u32[]{:S(2)}, u32[]{:S(2)}) collective-permute-start(bf16[2,128,128]{2,0,1:T(2,128)(2,1)S(1)} %get-tuple-element.46), channel_id=1, source_target_pairs={{4,0},{8,4},{12,8},{16,12},{20,16},{24,20},{28,24},{32,28},{36,32}... | collective-permute-start | bytes 196616 | tf_op jit(solution)/shard_map/ppermute | solution.py:33
  32.0 3.3 copy-start.9
  35.2 1.2 copy-start.5
  329.1 2.2 copy-start.1
  331.4 1.2 copy-start.2
  331.5 1.4 copy-start.7
  331.5 1.4 copy-start.8
  332.7 1.1 copy-start.4
  332.8 1.2 copy-start.6
  333.5 1.3 copy-start.3
Sparse Core Ops, SparseCore 0:
  10.5 151.2 all-gather.2
